TPU v7x, 32 devices: a whole 2x2x4 slice. The times are simulated.
32 devices in a mesh: row: 4 (over y, x), col: 8 (over z, core).
Axes of the slice: x: 2, y: 2, z: 4, core: 2. Of those that a mesh axis runs over, the one named last changes fastest.
Arguments:
- matrix: float32 [16384, 16384], P('row', 'col'), may hold values from -6 to 6
- factor_inverse: float32 [512, 512], replicated, may hold values from -0.25 to 0.25
- panel: int32 [1], replicated, may hold values from 0 to 31
- split_index: int32 [1], replicated, may hold values from 4096 to 12288
Outputs:
- halves: float32 [16384, 512], P('col')
All inputs are finite; a program needn't handle non-finite values.
Results may differ from a plain program's by a relative error of at most 0.000071.
Values sent between devices are 32-bit elements; how exact they have to be, the bound alone decides.
A program may use at most 128 MiB of HBM per device.

v0:
```python
import functools

import jax
import jax.numpy as jnp
from jax import lax
from jax.experimental import pallas as pl
from jax.experimental.pallas import tpu as pltpu
from jax.sharding import PartitionSpec as P

GROUPS = 2
CHUNKS = 16
VMEM_LIMIT = 40 * 1024 * 1024


def remote(src, dst, send, recv, target):
    return pltpu.make_async_remote_copy(
        src_ref=src,
        dst_ref=dst,
        send_sem=send,
        recv_sem=recv,
        device_id=target,
        device_id_type=pl.DeviceIdType.MESH,
    )


def signal(barrier, target):
    pl.semaphore_signal(barrier, inc=1, device_id=target, device_id_type=pl.DeviceIdType.MESH)


def spread_kernel(
    line, chunk, x_ref, o_ref, ex, rin, lin,
    ex_send, ex_recv, r_send, r_recv, l_send, l_recv, s_send, s_recv,
):
    c = lax.axis_index("col")
    z = c // 2
    k = c % 2
    half = CHUNKS * chunk
    base = pl.multiple_of(k * half, half)
    other = pl.multiple_of((1 - k) * half, half)
    sibling, up, down = {"col": c + 1 - 2 * k}, {"col": c + 2}, {"col": c - 2}
    has_down, has_up = z > 0, z < line - 1

    barrier = pltpu.get_barrier_semaphore()
    signal(barrier, sibling)

    @pl.when(has_down)
    def _():
        signal(barrier, down)

    @pl.when(has_up)
    def _():
        signal(barrier, up)

    pl.semaphore_wait(barrier, 1 + has_down.astype(jnp.int32) + has_up.astype(jnp.int32))

    swap = remote(x_ref.at[pl.ds(other, half)], ex, ex_send, ex_recv, sibling)
    swap.start()
    swap.wait()

    def rows_of(i):
        return pl.ds(pl.multiple_of(i * chunk, chunk), chunk)

    def whole_rows(i):
        return pl.ds(pl.multiple_of(base + i * chunk, chunk), chunk)

    def up_copy(i):
        return remote(rin.at[rows_of(i)], rin.at[rows_of(i)], r_send.at[i], r_recv.at[i], up)

    def down_copy(i):
        return remote(lin.at[rows_of(i)], lin.at[rows_of(i)], l_send.at[i], l_recv.at[i], down)

    def side_copy(i):
        return remote(
            o_ref.at[whole_rows(i)], o_ref.at[whole_rows(i)], s_send.at[i], s_recv.at[i], sibling
        )

    def own(i):
        return x_ref[whole_rows(i), :] + ex[rows_of(i), :]

    last = jnp.maximum(z, line - 1 - z)

    def step(t, carry):
        i = t - z

        @pl.when((i >= 0) & (i < CHUNKS))
        def _():
            @pl.when(z == 0)
            def _():
                rin[rows_of(i), :] = own(i)

            @pl.when(has_down)
            def _():
                up_copy(i).wait_recv()
                rin[rows_of(i), :] = rin[rows_of(i), :] + own(i)

            @pl.when(has_up)
            def _():
                up_copy(i).start()

        j = t - (line - 1 - z)

        @pl.when((j >= 0) & (j < CHUNKS))
        def _():
            @pl.when(z == line - 1)
            def _():
                lin[rows_of(j), :] = own(j)

            @pl.when(has_up)
            def _():
                down_copy(j).wait_recv()
                lin[rows_of(j), :] = lin[rows_of(j), :] + own(j)

            @pl.when(has_down)
            def _():
                down_copy(j).start()

        m = t - last

        @pl.when((m >= 0) & (m < CHUNKS))
        def _():
            o_ref[whole_rows(m), :] = (rin[rows_of(m), :] + lin[rows_of(m), :]) - own(m)
            side_copy(m).start()

        return carry

    lax.fori_loop(0, CHUNKS + line - 1, step, 0)

    def finish(i, carry):
        @pl.when(has_up)
        def _():
            up_copy(i).wait_send()

        @pl.when(has_down)
        def _():
            down_copy(i).wait_send()

        side_copy(i).wait_send()
        remote(
            o_ref.at[pl.ds(pl.multiple_of(other + i * chunk, chunk), chunk)],
            o_ref.at[pl.ds(pl.multiple_of(other + i * chunk, chunk), chunk)],
            s_send.at[i], s_recv.at[i], sibling,
        ).wait_recv()
        return carry

    lax.fori_loop(0, CHUNKS, finish, 0)


def spread(x, line):
    rows, cols = x.shape
    half = rows // 2
    chunk = half // CHUNKS
    buffer = pltpu.VMEM((half, cols), jnp.float32)
    return pl.pallas_call(
        functools.partial(spread_kernel, line, chunk),
        out_shape=jax.ShapeDtypeStruct((rows, cols), jnp.float32),
        in_specs=[pl.BlockSpec(memory_space=pltpu.VMEM)],
        out_specs=pl.BlockSpec(memory_space=pltpu.VMEM),
        scratch_shapes=[buffer] * 3
        + [pltpu.SemaphoreType.DMA] * 2
        + [pltpu.SemaphoreType.DMA((CHUNKS,))] * 6,
        compiler_params=pltpu.CompilerParams(
            collective_id=1, has_side_effects=True, vmem_limit_bytes=VMEM_LIMIT
        ),
        cost_estimate=pl.CostEstimate(flops=0, bytes_accessed=160 * 1000000, transcendentals=0),
        name="spread_panel",
    )(x)


def collect_kernel(
    line, chunk, p_ref, o_ref, ex, rin, lin,
    ex_send, ex_recv, z_send, r_recv, l_recv, a_send, b_send, o_recv, *more_send,
):
    r = lax.axis_index("row")
    c = lax.axis_index("col")
    z = c // 2
    k = c % 2
    half = CHUNKS * chunk
    base = pl.multiple_of(k * half, half)
    other = pl.multiple_of((1 - k) * half, half)
    sibling, up, down = {"col": c + 1 - 2 * k}, {"col": c + 2}, {"col": c - 2}
    square = line == 4
    is_root = r == z
    if square:
        across_x, across_y = {"row": r + 1 - 2 * (r % 2)}, {"row": r + 2 - 4 * (r // 2)}
        same_x, same_y = (r % 2) == (z % 2), (r // 2) == (z // 2)
        is_x = jnp.logical_not(same_x) & same_y
        is_y = same_x & jnp.logical_not(same_y)
        is_far = jnp.logical_not(same_x) & jnp.logical_not(same_y)

    barrier = pltpu.get_barrier_semaphore()
    signal(barrier, sibling)

    @pl.when((z > 0) & (z <= r))
    def _():
        signal(barrier, down)

    @pl.when((z < line - 1) & (z >= r))
    def _():
        signal(barrier, up)

    if square:
        @pl.when(is_x | is_far)
        def _():
            signal(barrier, across_x)

        @pl.when(is_y | is_far)
        def _():
            signal(barrier, across_y)
    else:
        @pl.when(jnp.logical_not(is_root))
        def _():
            signal(barrier, {"row": z})

    if square:
        pl.semaphore_wait(barrier, jnp.where(is_far, 2, 3))
    else:
        pl.semaphore_wait(barrier, jnp.where(is_root, line, 2))

    swap = remote(p_ref.at[pl.ds(other, half)], ex, ex_send, ex_recv, sibling)
    swap.start()
    swap.wait()

    def rows_of(i):
        return pl.ds(pl.multiple_of(i * chunk, chunk), chunk)

    def own(i):
        return p_ref[pl.ds(pl.multiple_of(base + i * chunk, chunk), chunk), :] + ex[rows_of(i), :]

    def up_copy(i):
        return remote(rin.at[rows_of(i)], rin.at[rows_of(i)], z_send.at[i], r_recv.at[i], up)

    def down_copy(i):
        return remote(lin.at[rows_of(i)], lin.at[rows_of(i)], z_send.at[i], l_recv.at[i], down)

    def out_copy(i, sems, target):
        return remote(o_ref.at[rows_of(i)], o_ref.at[rows_of(i)], sems.at[i], o_recv.at[i], target)

    last = jnp.maximum(z, line - 1 - z)

    def within(i):
        return (i >= 0) & (i < CHUNKS)

    def step(t, carry):
        i = t - z

        @pl.when(within(i) & (z < r))
        def _():
            @pl.when(z == 0)
            def _():
                rin[rows_of(i), :] = own(i)

            @pl.when(z > 0)
            def _():
                up_copy(i).wait_recv()
                rin[rows_of(i), :] = rin[rows_of(i), :] + own(i)

            up_copy(i).start()

        j = t - (line - 1 - z)

        @pl.when(within(j) & (z > r))
        def _():
            @pl.when(z == line - 1)
            def _():
                lin[rows_of(j), :] = own(j)

            @pl.when(z < line - 1)
            def _():
                down_copy(j).wait_recv()
                lin[rows_of(j), :] = lin[rows_of(j), :] + own(j)

            down_copy(j).start()

        m = t - last

        @pl.when(within(m) & is_root)
        def _():
            o_ref[rows_of(m), :] = own(m)

            @pl.when(z > 0)
            def _():
                up_copy(m).wait_recv()
                o_ref[rows_of(m), :] = o_ref[rows_of(m), :] + rin[rows_of(m), :]

            @pl.when(z < line - 1)
            def _():
                down_copy(m).wait_recv()
                o_ref[rows_of(m), :] = o_ref[rows_of(m), :] + lin[rows_of(m), :]

            if square:
                out_copy(m, a_send, across_x).start()
                out_copy(m, b_send, across_y).start()
            else:
                for n in range(1, line):
                    out_copy(m, more_send[n - 1], {"row": (z + n) % line}).start()

        if square:
            f = m - 1

            @pl.when(within(f) & is_x)
            def _():
                out_copy(f, a_send, across_y).wait_recv()

                @pl.when(f % 2 == 0)
                def _():
                    out_copy(f, a_send, across_y).start()

            @pl.when(within(f) & is_y)
            def _():
                out_copy(f, a_send, across_x).wait_recv()

                @pl.when(f % 2 == 1)
                def _():
                    out_copy(f, a_send, across_x).start()

        return carry

    lax.fori_loop(0, CHUNKS + line, step, 0)

    def finish(i, carry):
        @pl.when(jnp.logical_not(is_root))
        def _():
            up_copy(i).wait_send()

        if square:
            @pl.when(is_root)
            def _():
                out_copy(i, a_send, across_x).wait_send()
                out_copy(i, b_send, across_y).wait_send()

            @pl.when((is_x & (i % 2 == 0)) | (is_y & (i % 2 == 1)))
            def _():
                out_copy(i, a_send, across_y).wait_send()

            @pl.when(is_far)
            def _():
                out_copy(i, a_send, across_y).wait_recv()
        else:
            @pl.when(is_root)
            def _():
                for n in range(1, line):
                    out_copy(i, more_send[n - 1], {"row": (z + n) % line}).wait_send()

            @pl.when(jnp.logical_not(is_root))
            def _():
                out_copy(i, more_send[0], {"row": z}).wait_recv()

        return carry

    lax.fori_loop(0, CHUNKS, finish, 0)


def collect(p, line):
    rows, cols = p.shape
    half = rows // 2
    chunk = half // CHUNKS
    buffer = pltpu.VMEM((half, cols), jnp.float32)
    extra = 0 if line == 4 else line - 1
    return pl.pallas_call(
        functools.partial(collect_kernel, line, chunk),
        out_shape=jax.ShapeDtypeStruct((half, cols), jnp.float32),
        in_specs=[pl.BlockSpec(memory_space=pltpu.VMEM)],
        out_specs=pl.BlockSpec(memory_space=pltpu.VMEM),
        scratch_shapes=[buffer] * 3
        + [pltpu.SemaphoreType.DMA] * 2
        + [pltpu.SemaphoreType.DMA((CHUNKS,))] * (6 + extra),
        compiler_params=pltpu.CompilerParams(
            collective_id=2, has_side_effects=True, vmem_limit_bytes=VMEM_LIMIT
        ),
        cost_estimate=pl.CostEstimate(flops=0, bytes_accessed=160 * 1000000, transcendentals=0),
        name="collect_product",
    )(p)


def product(a, b, dims):
    return lax.dot_general(
        a, b, (dims, ((), ())), precision=lax.Precision.HIGH, preferred_element_type=jnp.float32
    )


def identity_rows(first, count, start, width):
    rows_global = first + jnp.arange(count, dtype=jnp.int32)
    return (rows_global[:, None] == start + jnp.arange(width, dtype=jnp.int32)[None, :]).astype(
        jnp.float32
    )


def per_device(matrix, factor_inverse, panel, split_index):
    cols_loc = matrix.shape[1]
    width = factor_inverse.shape[0]
    ncol = lax.axis_size("col")
    line = lax.axis_size("row")
    assert ncol == 2 * line
    order = cols_loc * ncol
    col_idx = lax.axis_index("col")
    start = panel[0] * width
    owner = start // cols_loc
    offset = start - owner * cols_loc
    group = width // GROUPS

    partials, grams, collected = [], [], []
    for g in range(GROUPS):
        piece = lax.dynamic_slice_in_dim(matrix, offset + g * group, group, 1)
        piece = jnp.where(owner == col_idx, piece, jnp.float32(0.0))
        if partials:
            piece, partials[-1] = lax.optimization_barrier((piece, partials[-1]))
        columns = spread(piece, line)
        partials.append(product(matrix, columns, ((0,), (0,))))
    for g in range(GROUPS):
        if grams:
            partials[g], grams[-1] = lax.optimization_barrier((partials[g], grams[-1]))
        grams.append(
            lax.psum(partials[g], "row") / order
            + identity_rows(col_idx * cols_loc, cols_loc, start + g * group, group)
        )
    for g in range(GROUPS):
        collected.append(collect(product(matrix, grams[g], ((1,), (0,))), line))
    total = product(jnp.concatenate(collected, axis=1), factor_inverse, ((1,), (1,)))
    col_rows = order // ncol
    projector = 0.5 * (identity_rows(col_idx * col_rows, col_rows, start, width) + total)
    rows_global = col_idx * col_rows + jnp.arange(col_rows, dtype=jnp.int32)
    keep = (rows_global < order // 2) == (rows_global < split_index[0])
    return jnp.where(keep[:, None], projector, jnp.float32(0.0))


def solution(mesh):
    placed = (P("row", "col"), P(), P(), P())
    return jax.shard_map(
        per_device, mesh=mesh, in_specs=placed, out_specs=P("col", None), check_vma=False
    )
```

profile of v0, /device:TPU:6, one launch (start us, length us, event | category | flops | bytes accessed | tf_op | source)
XLA Modules:
  0.0 447.2 jit_solution(2302277070879425691)
XLA Ops:
  6.5 0.0 copy-start
  6.5 0.0 all-reduce.3.cloned.1.call-start
  7.3 6.0 %dynamic-slice_select_fusion = (f32[4096,256]{1,0:T(8,128)S(1)}, f32[4096,256]{1,0:T(8,128)}) fusion(f32[4096,2048]{1,0:T(8,128)} %param.4, s32[]{:T(128)S(6)} %select_n.31, pred[]{:T(512)S(6)} %eq.52, s32[]{:T(128)S(6)} %select_n.29), kind=kLoop, calls=%fused_computation.7 | loop fusion | flops 2097152 | bytes 16777224 | tf_op jit(solution)/shard_map/jit(_where)/select_n | solution.py:404
  13.4 80.6 %spread_panel.2 = f32[4096,256]{1,0:T(8,128)S(1)} custom-call(f32[4096,256]{1,0:T(8,128)S(1)} %get-tuple-element.13.x_ref), custom_call_target="tpu_custom_call" | custom-call | bytes 160000000 | tf_op jit(solution)/shard_map/spread_panel/pallas_call | solution.py:153
  94.0 0.0 copy-start.4
  94.0 1.9 copy-done.4
  95.9 19.4 %convolution_bitcast_fusion.3 = f32[2048,256]{0,1:T(8,128)} fusion(f32[4096,256]{1,0:T(8,128)} %copy-done.4, f32[4096,2048]{1,0:T(8,128)} %param.4), kind=kOutput, calls=%fused_computation.10 | convolution fusion | flops 12884901888 | bytes 39845888 | tf_op jit(solution)/shard_map/dot_general | solution.py:376
  115.4 0.0 all-reduce.3.cloned.1.call-update
  115.4 0.0 all-reduce.5.cloned.1.call-start
  115.5 0.0 copy-start.1
  115.5 2.2 copy-done.1
  117.7 79.9 %spread_panel.3 = f32[4096,256]{1,0:T(8,128)S(1)} custom-call(f32[4096,256]{1,0:T(8,128)S(1)} %copy-done.1), custom_call_target="tpu_custom_call" | custom-call | bytes 160000000 | tf_op jit(solution)/shard_map/spread_panel/pallas_call | solution.py:153
  197.5 0.0 copy-start.2
  197.5 2.0 copy-done.2
  200.2 19.5 %convolution_bitcast_fusion.2 = f32[2048,256]{0,1:T(8,128)} fusion(f32[4096,256]{1,0:T(8,128)} %copy-done.2, f32[4096,2048]{1,0:T(8,128)} %param.4), kind=kOutput, calls=%fused_computation.9 | convolution fusion | flops 12884901888 | bytes 39845888 | tf_op jit(solution)/shard_map/dot_general | solution.py:376
  219.7 0.0 all-reduce.3.cloned.1.call-done
  219.7 1.9 convert_add_fusion
  221.6 0.0 all-reduce.5.cloned.1.call-update
  221.7 19.3 %convolution_bitcast_fusion.1.p_ref = f32[4096,256]{1,0:T(8,128)} fusion(f32[2048,256]{0,1:T(8,128)S(1)} %convert_add_fusion, f32[4096,2048]{1,0:T(8,128)} %param.4), kind=kOutput, calls=%fused_computation.1 | convolution fusion | flops 12884901888 | bytes 39845888 | tf_op jit(solution)/shard_map/dot_general | solution.py:376
  241.0 0.0 copy-start.5
  241.0 2.2 copy-done.5
  243.2 90.4 %collect_product.2 = f32[2048,256]{1,0:T(8,128)S(1)} custom-call(f32[4096,256]{1,0:T(8,128)S(1)} %copy-done.5), custom_call_target="tpu_custom_call" | custom-call | bytes 160000000 | tf_op jit(solution)/shard_map/collect_product/pallas_call | solution.py:359
  333.5 0.0 all-reduce.5.cloned.1.call-done
  333.6 22.1 %convolution_bitcast_fusion.p_ref = f32[4096,256]{1,0:T(8,128)} fusion(f32[4096,2048]{1,0:T(8,128)} %param.4, f32[2048,256]{0,1:T(8,128)} %all-reduce.5.cloned.1.call-done, s32[2048]{0:T(1024)S(1)} %iota_add_fusion, s32[256]{0:T(256)S(1)} %iota_add_fusion.2), kind=kOutput, calls=%fused_computation | convolution fusion | flops 12886999040 | bytes 39855104 | tf_op jit(solution)/shard_map/dot_general | solution.py:376
  355.6 0.0 copy-start.3
  355.6 2.2 copy-done.3
  357.8 76.8 %collect_product.3 = f32[2048,256]{1,0:T(8,128)S(1)} custom-call(f32[4096,256]{1,0:T(8,128)S(1)} %copy-done.3), custom_call_target="tpu_custom_call" | custom-call | bytes 160000000 | tf_op jit(solution)/shard_map/collect_product/pallas_call | solution.py:359
  434.7 0.0 copy-done
  434.7 5.7 %multiply_select_fusion = f32[2048,512]{1,0:T(8,128)} fusion(f32[512,512]{1,0:T(8,128)S(1)} %copy-done, f32[2048,256]{1,0:T(8,128)S(1)} %collect_product.3, f32[2048,256]{1,0:T(8,128)S(1)} %collect_product.2, s32[512]{0:T(512)S(1)} %iota_add_fusion.1, s32[2048]{0:T(1024)S(1)} %iota_add_fusion, pred[2048]{0:T(1024)(128)(4,1)S(1)} %compare_compare_fusion), kind=kOutput, calls=%fused_computation.6 | convolution fusion | flops 3227516928 | bytes 9449472 | tf_op jit(solution)/shard_map/dot_general | solution.py:376
  (5 shorter events, 0.0 us)
Async XLA Ops:
  6.5 428.1 %copy-start = (f32[512,512]{1,0:T(8,128)S(1)}, f32[512,512]{1,0:T(8,128)}, u32[]{:S(2)}) copy-start(f32[512,512]{1,0:T(8,128)} %param.5) | copy-start | bytes 3145732
  6.5 213.1 %all-reduce.3.cloned.1.call-start = ((), (), s32[]{:S(2)}) async-start(), calls=%async_computation | async-start | bytes 4194304 | tf_op jit(solution)/shard_map/psum | solution.py:413
  94.0 1.9 copy-start.4
  115.4 218.1 %all-reduce.5.cloned.1.call-start = ((), (), s32[]{:S(2)}) async-start(), calls=%async_computation.1 | async-start | bytes 4194304 | tf_op jit(solution)/shard_map/psum | solution.py:413
  115.5 2.2 copy-start.1
  197.5 2.0 copy-start.2
  241.0 2.2 copy-start.5
  355.6 2.2 copy-start.3
Sparse Core Ops, SparseCore 0:
  115.5 68.0 all-reduce.2
  221.8 75.2 all-reduce.4
where the time goes:
time: 448 us; the launch traced here: 447 us
  Pallas kernels  328 us (73%)
  matrix products  86 us (19%)
  between operations  14.9 us (3%)
  local copies, waits for them, and re-layouts  10.5 us (2%)
  other arithmetic  8 us (2%)
    pallas_call x2, Pallas kernels, collect(): pl.pallas_call(functools.partial(collect_kernel, line, chunk), out_shape=...  167 us
    pallas_call x2, Pallas kernels, spread(): pl.pallas_call(functools.partial(spread_kernel, line, chunk), out_shape=j...  160 us
    dot_general x5, matrix products, product(): lax.dot_general(a, b, (dims, ((), ())), precision=lax.Precision.HIGH, pre...  86 us
    unnamed x12, local copies, waits for them, and re-layouts  10.5 us
  transfers between devices with their start and end apart: 2, of which 0 were waited for; matrix products, arithmetic and copies ran while one was open for 9% of the time, Pallas kernels for 38%

commit v1 on v0

--- a/solution.py
+++ b/solution.py
@@ -8,7 +8,8 @@
 from jax.sharding import PartitionSpec as P
 
 GROUPS = 2
-CHUNKS = 16
+CHUNKS = 32
+SKEW = 3
 VMEM_LIMIT = 40 * 1024 * 1024
 
 
@@ -80,7 +81,7 @@
     last = jnp.maximum(z, line - 1 - z)
 
     def step(t, carry):
-        i = t - z
+        i = t - SKEW * z
 
         @pl.when((i >= 0) & (i < CHUNKS))
         def _():
@@ -97,7 +98,7 @@
             def _():
                 up_copy(i).start()
 
-        j = t - (line - 1 - z)
+        j = t - SKEW * (line - 1 - z)
 
         @pl.when((j >= 0) & (j < CHUNKS))
         def _():
@@ -114,7 +115,7 @@
             def _():
                 down_copy(j).start()
 
-        m = t - last
+        m = t - SKEW * last
 
         @pl.when((m >= 0) & (m < CHUNKS))
         def _():
@@ -123,7 +124,7 @@
 
         return carry
 
-    lax.fori_loop(0, CHUNKS + line - 1, step, 0)
+    lax.fori_loop(0, CHUNKS + SKEW * (line - 1), step, 0)
 
     def finish(i, carry):
         @pl.when(has_up)
@@ -241,7 +242,7 @@
         return (i >= 0) & (i < CHUNKS)
 
     def step(t, carry):
-        i = t - z
+        i = t - SKEW * z
 
         @pl.when(within(i) & (z < r))
         def _():
@@ -256,7 +257,7 @@
 
             up_copy(i).start()
 
-        j = t - (line - 1 - z)
+        j = t - SKEW * (line - 1 - z)
 
         @pl.when(within(j) & (z > r))
         def _():
@@ -271,7 +272,7 @@
 
             down_copy(j).start()
 
-        m = t - last
+        m = t - SKEW * last
 
         @pl.when(within(m) & is_root)
         def _():
@@ -295,7 +296,7 @@
                     out_copy(m, more_send[n - 1], {"row": (z + n) % line}).start()
 
         if square:
-            f = m - 1
+            f = m - SKEW
 
             @pl.when(within(f) & is_x)
             def _():
@@ -315,7 +316,7 @@
 
         return carry
 
-    lax.fori_loop(0, CHUNKS + line, step, 0)
+    lax.fori_loop(0, CHUNKS + SKEW * line, step, 0)
 
     def finish(i, carry):
         @pl.when(jnp.logical_not(is_root))

time: 448 us -> 395 us (0.88)
  Pallas kernels: 328 us -> 275 us
    pallas_call x2, Pallas kernels: 160 us -> 125 us  [spread(): pl.pallas_call(functools.partial(spread_kernel, line, chunk), out_shape=j...]
    pallas_call x2, Pallas kernels: 167 us -> 150 us  [collect(): pl.pallas_call(functools.partial(collect_kernel, line, chunk), out_shape=...]
  transfers between devices with their start and end apart: 2 -> 2, of which waited for: 0 -> 0; matrix products, arithmetic and copies ran while one was open for 9% -> 10% of each run, Pallas kernels for 38% -> 36%
where the time goes in v1:
time: 395 us; the launch traced here: 394 us
  Pallas kernels  275 us (70%)
  matrix products  86 us (22%)
  between operations  14.9 us (4%)
  local copies, waits for them, and re-layouts  10.5 us (3%)
  other arithmetic  8 us (2%)
    pallas_call x2, Pallas kernels, collect(): pl.pallas_call(functools.partial(collect_kernel, line, chunk), out_shape=...  150 us
    pallas_call x2, Pallas kernels, spread(): pl.pallas_call(functools.partial(spread_kernel, line, chunk), out_shape=j...  125 us
    dot_general x5, matrix products, product(): lax.dot_general(a, b, (dims, ((), ())), precision=lax.Precision.HIGH, pre...  86 us
    unnamed x12, local copies, waits for them, and re-layouts  10.5 us
  transfers between devices with their start and end apart: 2, of which 0 were waited for; matrix products, arithmetic and copies ran while one was open for 10% of the time, Pallas kernels for 36%

profile of v1, /device:TPU:6, one launch (start us, length us, event | category | flops | bytes accessed | tf_op | source)
XLA Modules:
  0.0 394.0 jit_solution(7932561286625201369)
XLA Ops:
  6.5 0.0 copy-start
  6.5 0.0 all-reduce.3.cloned.1.call-start
  7.3 6.0 %dynamic-slice_select_fusion = (f32[4096,256]{1,0:T(8,128)S(1)}, f32[4096,256]{1,0:T(8,128)}) fusion(f32[4096,2048]{1,0:T(8,128)} %param.4, s32[]{:T(128)S(6)} %select_n.31, pred[]{:T(512)S(6)} %eq.52, s32[]{:T(128)S(6)} %select_n.29), kind=kLoop, calls=%fused_computation.7 | loop fusion | flops 2097152 | bytes 16777224 | tf_op jit(solution)/shard_map/jit(_where)/select_n | solution.py:405
  13.4 63.2 %spread_panel.2 = f32[4096,256]{1,0:T(8,128)S(1)} custom-call(f32[4096,256]{1,0:T(8,128)S(1)} %get-tuple-element.13.x_ref), custom_call_target="tpu_custom_call" | custom-call | bytes 160000000 | tf_op jit(solution)/shard_map/spread_panel/pallas_call | solution.py:154
  76.5 0.0 copy-start.4
  76.5 1.9 copy-done.4
  78.5 19.4 %convolution_bitcast_fusion.3 = f32[2048,256]{0,1:T(8,128)} fusion(f32[4096,256]{1,0:T(8,128)} %copy-done.4, f32[4096,2048]{1,0:T(8,128)} %param.4), kind=kOutput, calls=%fused_computation.10 | convolution fusion | flops 12884901888 | bytes 39845888 | tf_op jit(solution)/shard_map/dot_general | solution.py:377
  97.9 0.0 all-reduce.3.cloned.1.call-update
  98.0 0.0 all-reduce.5.cloned.1.call-start
  98.0 0.0 copy-start.1
  98.0 2.2 copy-done.1
  100.2 61.8 %spread_panel.3 = f32[4096,256]{1,0:T(8,128)S(1)} custom-call(f32[4096,256]{1,0:T(8,128)S(1)} %copy-done.1), custom_call_target="tpu_custom_call" | custom-call | bytes 160000000 | tf_op jit(solution)/shard_map/spread_panel/pallas_call | solution.py:154
  162.0 0.0 copy-start.2
  162.1 2.0 copy-done.2
  164.7 19.5 %convolution_bitcast_fusion.2 = f32[2048,256]{0,1:T(8,128)} fusion(f32[4096,256]{1,0:T(8,128)} %copy-done.2, f32[4096,2048]{1,0:T(8,128)} %param.4), kind=kOutput, calls=%fused_computation.9 | convolution fusion | flops 12884901888 | bytes 39845888 | tf_op jit(solution)/shard_map/dot_general | solution.py:377
  184.2 0.0 all-reduce.3.cloned.1.call-done
  184.2 1.9 convert_add_fusion
  186.1 0.0 all-reduce.5.cloned.1.call-update
  186.2 19.3 %convolution_bitcast_fusion.1.p_ref = f32[4096,256]{1,0:T(8,128)} fusion(f32[2048,256]{0,1:T(8,128)S(1)} %convert_add_fusion, f32[4096,2048]{1,0:T(8,128)} %param.4), kind=kOutput, calls=%fused_computation.1 | convolution fusion | flops 12884901888 | bytes 39845888 | tf_op jit(solution)/shard_map/dot_general | solution.py:377
  205.5 0.0 copy-start.5
  205.5 2.2 copy-done.5
  207.7 81.8 %collect_product.2 = f32[2048,256]{1,0:T(8,128)S(1)} custom-call(f32[4096,256]{1,0:T(8,128)S(1)} %copy-done.5), custom_call_target="tpu_custom_call" | custom-call | bytes 160000000 | tf_op jit(solution)/shard_map/collect_product/pallas_call | solution.py:360
  289.5 0.0 all-reduce.5.cloned.1.call-done
  289.5 22.1 %convolution_bitcast_fusion.p_ref = f32[4096,256]{1,0:T(8,128)} fusion(f32[4096,2048]{1,0:T(8,128)} %param.4, f32[2048,256]{0,1:T(8,128)} %all-reduce.5.cloned.1.call-done, s32[2048]{0:T(1024)S(1)} %iota_add_fusion, s32[256]{0:T(256)S(1)} %iota_add_fusion.2), kind=kOutput, calls=%fused_computation | convolution fusion | flops 12886999040 | bytes 39855104 | tf_op jit(solution)/shard_map/dot_general | solution.py:377
  311.6 0.0 copy-start.3
  311.6 2.2 copy-done.3
  313.8 67.7 %collect_product.3 = f32[2048,256]{1,0:T(8,128)S(1)} custom-call(f32[4096,256]{1,0:T(8,128)S(1)} %copy-done.3), custom_call_target="tpu_custom_call" | custom-call | bytes 160000000 | tf_op jit(solution)/shard_map/collect_product/pallas_call | solution.py:360
  381.5 0.0 copy-done
  381.5 5.7 %multiply_select_fusion = f32[2048,512]{1,0:T(8,128)} fusion(f32[512,512]{1,0:T(8,128)S(1)} %copy-done, f32[2048,256]{1,0:T(8,128)S(1)} %collect_product.3, f32[2048,256]{1,0:T(8,128)S(1)} %collect_product.2, s32[512]{0:T(512)S(1)} %iota_add_fusion.1, s32[2048]{0:T(1024)S(1)} %iota_add_fusion, pred[2048]{0:T(1024)(128)(4,1)S(1)} %compare_compare_fusion), kind=kOutput, calls=%fused_computation.6 | convolution fusion | flops 3227516928 | bytes 9449472 | tf_op jit(solution)/shard_map/dot_general | solution.py:377
  (5 shorter events, 0.0 us)
Async XLA Ops:
  6.5 375.0 %copy-start = (f32[512,512]{1,0:T(8,128)S(1)}, f32[512,512]{1,0:T(8,128)}, u32[]{:S(2)}) copy-start(f32[512,512]{1,0:T(8,128)} %param.5) | copy-start | bytes 3145732
  6.5 177.7 %all-reduce.3.cloned.1.call-start = ((), (), s32[]{:S(2)}) async-start(), calls=%async_computation | async-start | bytes 4194304 | tf_op jit(solution)/shard_map/psum | solution.py:414
  76.5 1.9 copy-start.4
  98.0 191.5 %all-reduce.5.cloned.1.call-start = ((), (), s32[]{:S(2)}) async-start(), calls=%async_computation.1 | async-start | bytes 4194304 | tf_op jit(solution)/shard_map/psum | solution.py:414
  98.0 2.2 copy-start.1
  162.0 2.0 copy-start.2
  205.5 2.2 copy-start.5
  311.6 2.2 copy-start.3
Sparse Core Ops, SparseCore 0:
  98.1 67.5 all-reduce.2
  186.3 77.5 all-reduce.4

commit v2 on v1

--- a/solution.py
+++ b/solution.py
@@ -10,6 +10,8 @@
 GROUPS = 2
 CHUNKS = 32
 SKEW = 3
+BLOCKS = 4
+EACH = CHUNKS // BLOCKS
 VMEM_LIMIT = 40 * 1024 * 1024
 
 
@@ -28,8 +30,19 @@
     pl.semaphore_signal(barrier, inc=1, device_id=target, device_id_type=pl.DeviceIdType.MESH)
 
 
+def parts_of(x):
+    high = x.astype(jnp.bfloat16)
+    return high, (x - high.astype(jnp.float32)).astype(jnp.bfloat16)
+
+
+def split_dot(a, b):
+    total = jnp.dot(a[1], b[0], preferred_element_type=jnp.float32)
+    total = total + jnp.dot(a[0], b[1], preferred_element_type=jnp.float32)
+    return total + jnp.dot(a[0], b[0], preferred_element_type=jnp.float32)
+
+
 def spread_kernel(
-    line, chunk, x_ref, o_ref, ex, rin, lin,
+    line, chunk, x_ref, a_ref, g_ref, o_ref, a_buf, a_sem, ex, rin, lin,
     ex_send, ex_recv, r_send, r_recv, l_send, l_recv, s_send, s_recv,
 ):
     c = lax.axis_index("col")
@@ -54,6 +67,29 @@
 
     pl.semaphore_wait(barrier, 1 + has_down.astype(jnp.int32) + has_up.astype(jnp.int32))
 
+    block = EACH * chunk
+
+    def block_rows(q):
+        half_no = (k + q) % 2
+        return pl.ds(pl.multiple_of(half_no * half + (q // 2) * block, block), block)
+
+    def load(q):
+        slot = q % 2
+        return pltpu.make_async_copy(a_ref.at[block_rows(q)], a_buf.at[slot], a_sem.at[slot])
+
+    load(0).start()
+    load(1).start()
+    g_ref[...] = jnp.zeros_like(g_ref)
+
+    def accumulate(q):
+        load(q).wait()
+        panel = parts_of(jnp.transpose(o_ref[block_rows(q), :]))
+        g_ref[...] += split_dot(panel, parts_of(a_buf[q % 2]))
+
+        @pl.when(q + 2 < 2 * BLOCKS)
+        def _():
+            load(q + 2).start()
+
     swap = remote(x_ref.at[pl.ds(other, half)], ex, ex_send, ex_recv, sibling)
     swap.start()
     swap.wait()
@@ -75,6 +111,18 @@
             o_ref.at[whole_rows(i)], o_ref.at[whole_rows(i)], s_send.at[i], s_recv.at[i], sibling
         )
 
+    def side_wait(i):
+        rows = pl.ds(pl.multiple_of(other + i * chunk, chunk), chunk)
+        remote(o_ref.at[rows], o_ref.at[rows], s_send.at[i], s_recv.at[i], sibling).wait_recv()
+
+    def accumulate_side(b):
+        def wait_one(n, carry):
+            side_wait(b * EACH + n)
+            return carry
+
+        lax.fori_loop(0, EACH, wait_one, 0)
+        accumulate(2 * b + 1)
+
     def own(i):
         return x_ref[whole_rows(i), :] + ex[rows_of(i), :]
 
@@ -122,9 +170,19 @@
             o_ref[whole_rows(m), :] = (rin[rows_of(m), :] + lin[rows_of(m), :]) - own(m)
             side_copy(m).start()
 
+            @pl.when(m % EACH == EACH - 1)
+            def _():
+                accumulate(2 * (m // EACH))
+
+            @pl.when((m % EACH == EACH // 2 - 1) & (m >= EACH))
+            def _():
+                accumulate_side(m // EACH - 1)
+
         return carry
 
     lax.fori_loop(0, CHUNKS + SKEW * (line - 1), step, 0)
+
+    accumulate_side(BLOCKS - 1)
 
     def finish(i, carry):
         @pl.when(has_up)
@@ -136,39 +194,42 @@
             down_copy(i).wait_send()
 
         side_copy(i).wait_send()
-        remote(
-            o_ref.at[pl.ds(pl.multiple_of(other + i * chunk, chunk), chunk)],
-            o_ref.at[pl.ds(pl.multiple_of(other + i * chunk, chunk), chunk)],
-            s_send.at[i], s_recv.at[i], sibling,
-        ).wait_recv()
         return carry
 
     lax.fori_loop(0, CHUNKS, finish, 0)
 
 
-def spread(x, line):
+def spread(x, matrix, line):
     rows, cols = x.shape
+    depth = matrix.shape[1]
     half = rows // 2
     chunk = half // CHUNKS
     buffer = pltpu.VMEM((half, cols), jnp.float32)
     return pl.pallas_call(
         functools.partial(spread_kernel, line, chunk),
-        out_shape=jax.ShapeDtypeStruct((rows, cols), jnp.float32),
-        in_specs=[pl.BlockSpec(memory_space=pltpu.VMEM)],
+        out_shape=jax.ShapeDtypeStruct((cols, depth), jnp.float32),
+        in_specs=[pl.BlockSpec(memory_space=pltpu.VMEM), pl.BlockSpec(memory_space=pl.ANY)],
         out_specs=pl.BlockSpec(memory_space=pltpu.VMEM),
-        scratch_shapes=[buffer] * 3
+        scratch_shapes=[
+            pltpu.VMEM((rows, cols), jnp.float32),
+            pltpu.VMEM((2, EACH * chunk, depth), jnp.float32),
+            pltpu.SemaphoreType.DMA((2,)),
+        ]
+        + [buffer] * 3
         + [pltpu.SemaphoreType.DMA] * 2
         + [pltpu.SemaphoreType.DMA((CHUNKS,))] * 6,
         compiler_params=pltpu.CompilerParams(
             collective_id=1, has_side_effects=True, vmem_limit_bytes=VMEM_LIMIT
         ),
-        cost_estimate=pl.CostEstimate(flops=0, bytes_accessed=160 * 1000000, transcendentals=0),
+        cost_estimate=pl.CostEstimate(
+            flops=6 * rows * cols * depth, bytes_accessed=220 * 1000000, transcendentals=0
+        ),
         name="spread_panel",
-    )(x)
+    )(x, matrix)
 
 
 def collect_kernel(
-    line, chunk, p_ref, o_ref, ex, rin, lin,
+    line, chunk, g_ref, a_ref, o_ref, a_buf, a_sem, g_high, g_low, p_own, p_other, ex, rin, lin,
     ex_send, ex_recv, z_send, r_recv, l_recv, a_send, b_send, o_recv, *more_send,
 ):
     r = lax.axis_index("row")
@@ -217,15 +278,43 @@
     else:
         pl.semaphore_wait(barrier, jnp.where(is_root, line, 2))
 
-    swap = remote(p_ref.at[pl.ds(other, half)], ex, ex_send, ex_recv, sibling)
-    swap.start()
-    swap.wait()
+    block = EACH * chunk
+
+    def load(q):
+        slot = q % 2
+        first = ((1 - k + q) % 2) * half + (q // 2) * block
+        rows = pl.ds(pl.multiple_of(first, block), block)
+        return pltpu.make_async_copy(a_ref.at[rows], a_buf.at[slot], a_sem.at[slot])
+
+    def block_rows(b):
+        return pl.ds(pl.multiple_of(b * block, block), block)
+
+    def multiply(q, target):
+        load(q).wait()
+        target[block_rows(q // 2), :] = split_dot(
+            parts_of(a_buf[q % 2]), (g_high[...], g_low[...])
+        )
+
+        @pl.when(q + 2 < 2 * BLOCKS)
+        def _():
+            load(q + 2).start()
+
+    def swap(b):
+        rows = block_rows(b)
+        return remote(p_other.at[rows], ex.at[rows], ex_send.at[b], ex_recv.at[b], sibling)
+
+    load(0).start()
+    load(1).start()
+    g_high[...], g_low[...] = parts_of(g_ref[...])
+    multiply(0, p_other)
+    swap(0).start()
+    multiply(1, p_own)
 
     def rows_of(i):
         return pl.ds(pl.multiple_of(i * chunk, chunk), chunk)
 
     def own(i):
-        return p_ref[pl.ds(pl.multiple_of(base + i * chunk, chunk), chunk), :] + ex[rows_of(i), :]
+        return p_own[rows_of(i), :] + ex[rows_of(i), :]
 
     def up_copy(i):
         return remote(rin.at[rows_of(i)], rin.at[rows_of(i)], z_send.at[i], r_recv.at[i], up)
@@ -242,6 +331,21 @@
         return (i >= 0) & (i < CHUNKS)
 
     def step(t, carry):
+        now = t // EACH
+
+        @pl.when((t % EACH == 0) & (now < BLOCKS))
+        def _():
+            swap(now).wait_recv()
+
+        @pl.when((t % EACH == 0) & (now < BLOCKS - 1))
+        def _():
+            multiply(2 * now + 2, p_other)
+            swap(now + 1).start()
+
+        @pl.when((t % EACH == EACH // 2) & (now < BLOCKS - 1))
+        def _():
+            multiply(2 * now + 3, p_own)
+
         i = t - SKEW * z
 
         @pl.when(within(i) & (z < r))
@@ -318,6 +422,9 @@
 
     lax.fori_loop(0, CHUNKS + SKEW * line, step, 0)
 
+    for b in range(BLOCKS):
+        swap(b).wait_send()
+
     def finish(i, carry):
         @pl.when(jnp.logical_not(is_root))
         def _():
@@ -351,26 +458,33 @@
     lax.fori_loop(0, CHUNKS, finish, 0)
 
 
-def collect(p, line):
-    rows, cols = p.shape
-    half = rows // 2
+def collect(gram, matrix, line):
+    depth, cols = gram.shape
+    half = matrix.shape[0] // 2
     chunk = half // CHUNKS
     buffer = pltpu.VMEM((half, cols), jnp.float32)
     extra = 0 if line == 4 else line - 1
     return pl.pallas_call(
         functools.partial(collect_kernel, line, chunk),
         out_shape=jax.ShapeDtypeStruct((half, cols), jnp.float32),
-        in_specs=[pl.BlockSpec(memory_space=pltpu.VMEM)],
+        in_specs=[pl.BlockSpec(memory_space=pltpu.VMEM), pl.BlockSpec(memory_space=pl.ANY)],
         out_specs=pl.BlockSpec(memory_space=pltpu.VMEM),
-        scratch_shapes=[buffer] * 3
-        + [pltpu.SemaphoreType.DMA] * 2
+        scratch_shapes=[
+            pltpu.VMEM((2, EACH * chunk, depth), jnp.float32),
+            pltpu.SemaphoreType.DMA((2,)),
+        ]
+        + [pltpu.VMEM((depth, cols), jnp.bfloat16)] * 2
+        + [buffer] * 5
+        + [pltpu.SemaphoreType.DMA((BLOCKS,))] * 2
         + [pltpu.SemaphoreType.DMA((CHUNKS,))] * (6 + extra),
         compiler_params=pltpu.CompilerParams(
             collective_id=2, has_side_effects=True, vmem_limit_bytes=VMEM_LIMIT
         ),
-        cost_estimate=pl.CostEstimate(flops=0, bytes_accessed=160 * 1000000, transcendentals=0),
+        cost_estimate=pl.CostEstimate(
+            flops=12 * half * cols * depth, bytes_accessed=220 * 1000000, transcendentals=0
+        ),
         name="collect_product",
-    )(p)
+    )(gram, matrix)
 
 
 def product(a, b, dims):
@@ -405,17 +519,16 @@
         piece = jnp.where(owner == col_idx, piece, jnp.float32(0.0))
         if partials:
             piece, partials[-1] = lax.optimization_barrier((piece, partials[-1]))
-        columns = spread(piece, line)
-        partials.append(product(matrix, columns, ((0,), (0,))))
+        partials.append(spread(piece, matrix, line))
     for g in range(GROUPS):
         if grams:
             partials[g], grams[-1] = lax.optimization_barrier((partials[g], grams[-1]))
         grams.append(
-            lax.psum(partials[g], "row") / order
+            lax.psum(partials[g], "row").T / order
             + identity_rows(col_idx * cols_loc, cols_loc, start + g * group, group)
         )
     for g in range(GROUPS):
-        collected.append(collect(product(matrix, grams[g], ((1,), (0,))), line))
+        collected.append(collect(grams[g], matrix, line))
     total = product(jnp.concatenate(collected, axis=1), factor_inverse, ((1,), (1,)))
     col_rows = order // ncol
     projector = 0.5 * (identity_rows(col_idx * col_rows, col_rows, start, width) + total)

time: 395 us -> 345 us (0.87)
  matrix products: 86 us -> 5.67 us
  Pallas kernels: 275 us -> 305 us
    dot_general x5 -> x1, matrix products: 86 us -> 5.67 us  [product(): lax.dot_general(a, b, (dims, ((), ())), precision=lax.Precision.HIGH, pre...]
    pallas_call x2, Pallas kernels: 150 us -> 172 us  [collect(): pl.pallas_call(functools.partial(collect_kernel, line, chunk), out_shape=...]
    pallas_call x2, Pallas kernels: 125 us -> 133 us  [spread(): pl.pallas_call(functools.partial(spread_kernel, line, chunk), out_shape=j...]
    unnamed x12 -> x10, local copies, waits for them, and re-layouts: 10.5 us -> 4.82 us
    optimization_barrier x0 -> x2, local copies, waits for them, and re-layouts: none -> 4.74 us  [the longest x1 2.91 us: per_device(): partials[g], grams[-1] = lax.optimization_barrier((partials[g], grams[-1]))]
  transfers between devices with their start and end apart: 2 -> 2, of which waited for: 0 -> 0; matrix products, arithmetic and copies ran while one was open for 10% -> 0% of each run, Pallas kernels for 36% -> 47%
where the time goes in v2:
time: 345 us
  Pallas kernels  305 us (88%)
  between operations  15 us (4%)
  other arithmetic  9.6 us (3%)
  local copies, waits for them, and re-layouts  9.56 us (3%)
  matrix products  5.67 us (2%)
    pallas_call x2, Pallas kernels, collect(): pl.pallas_call(functools.partial(collect_kernel, line, chunk), out_shape=...  172 us
    pallas_call x2, Pallas kernels, spread(): pl.pallas_call(functools.partial(spread_kernel, line, chunk), out_shape=j...  133 us
  transfers between devices with their start and end apart: 2, of which 0 were waited for; matrix products, arithmetic and copies ran while one was open for 0% of the time, Pallas kernels for 47%

profile of v2, /device:TPU:6, one launch (start us, length us, event | category | flops | bytes accessed | tf_op | source)
XLA Modules:
  0.0 345.0 jit_solution(16522122242560222527)
XLA Ops:
  6.5 0.0 copy-start
  6.5 0.0 all-reduce.3.cloned.1.call-start
  7.3 6.0 %dynamic-slice_select_fusion = (f32[4096,256]{1,0:T(8,128)S(1)}, f32[4096,256]{1,0:T(8,128)}) fusion(f32[4096,2048]{1,0:T(8,128)} %a_ref.7, s32[]{:T(128)S(6)} %select_n.31, pred[]{:T(512)S(6)} %eq.52, s32[]{:T(128)S(6)} %select_n.29), kind=kLoop, calls=%fused_computation.5 | loop fusion | flops 2097152 | bytes 16777224 | tf_op jit(solution)/shard_map/jit(_where)/select_n | solution.py:519
  13.4 67.8 %spread_panel.2 = f32[256,2048]{1,0:T(8,128)S(1)} custom-call(f32[4096,256]{1,0:T(8,128)S(1)} %get-tuple-element.13.x_ref, f32[4096,2048]{1,0:T(8,128)} %a_ref.7), custom_call_target="tpu_custom_call" | custom-call | flops 12884901888 | bytes 220000000 | tf_op jit(solution)/shard_map/spread_panel/pallas_call | solution.py:208
  81.2 1.8 copy.5
  83.0 0.0 all-reduce.3.cloned.1.call-update
  83.1 0.0 all-reduce.5.cloned.1.call-start
  83.1 0.0 copy-start.1
  83.1 2.2 copy-done.1
  85.3 65.5 %spread_panel.3 = f32[256,2048]{1,0:T(8,128)S(1)} custom-call(f32[4096,256]{1,0:T(8,128)S(1)} %copy-done.1, f32[4096,2048]{1,0:T(8,128)} %a_ref.7), custom_call_target="tpu_custom_call" | custom-call | flops 12884901888 | bytes 220000000 | tf_op jit(solution)/shard_map/spread_panel/pallas_call | solution.py:208
  150.8 0.0 copy-start.2
  150.9 1.3 copy-done.2
  152.2 0.0 all-reduce.3.cloned.1.call-done
  152.2 1.8 bitcast_add_fusion.1.g_ref
  153.9 2.9 copy.6
  156.8 0.0 all-reduce.5.cloned.1.call-update
  157.6 96.4 %collect_product.2 = f32[2048,256]{1,0:T(8,128)S(1)} custom-call(f32[2048,256]{1,0:T(8,128)S(1)} %bitcast_add_fusion.1.g_ref, f32[4096,2048]{1,0:T(8,128)} %a_ref.7), custom_call_target="tpu_custom_call" | custom-call | flops 12884901888 | bytes 220000000 | tf_op jit(solution)/shard_map/collect_product/pallas_call | solution.py:467
  254.0 0.0 copy-start.3
  254.0 1.3 copy-done.3
  255.3 0.0 all-reduce.5.cloned.1.call-done
  255.3 1.8 bitcast_add_fusion.g_ref
  257.1 0.0 copy-start.4
  257.1 75.4 %collect_product.3 = f32[2048,256]{1,0:T(8,128)S(1)} custom-call(f32[2048,256]{1,0:T(8,128)S(1)} %bitcast_add_fusion.g_ref, f32[4096,2048]{1,0:T(8,128)} %a_ref.7), custom_call_target="tpu_custom_call" | custom-call | flops 12884901888 | bytes 220000000 | tf_op jit(solution)/shard_map/collect_product/pallas_call | solution.py:467
  332.5 0.0 copy-done
  332.5 0.0 copy-done.4
  332.5 5.7 %multiply_select_fusion = f32[2048,512]{1,0:T(8,128)} fusion(f32[512,512]{1,0:T(8,128)S(1)} %copy-done, f32[2048,256]{1,0:T(8,128)S(1)} %collect_product.3, f32[2048,256]{1,0:T(8,128)S(1)} %copy-done.4, s32[512]{0:T(512)S(1)} %iota_add_fusion.1, s32[2048]{0:T(1024)S(1)} %iota_add_fusion, pred[2048]{0:T(1024)(128)(4,1)S(1)} %compare_compare_fusion), kind=kOutput, calls=%fused_computation.4 | convolution fusion | flops 3227516928 | bytes 9449472 | tf_op jit(solution)/shard_map/dot_general | solution.py:491
  (5 shorter events, 0.0 us)
Async XLA Ops:
  6.5 326.0 %copy-start = (f32[512,512]{1,0:T(8,128)S(1)}, f32[512,512]{1,0:T(8,128)}, u32[]{:S(2)}) copy-start(f32[512,512]{1,0:T(8,128)} %param.5) | copy-start | bytes 3145732
  6.5 145.6 %all-reduce.3.cloned.1.call-start = ((), (), s32[]{:S(2)}) async-start(), calls=%async_computation | async-start | bytes 4194304 | tf_op jit(solution)/shard_map/psum | solution.py:527
  83.1 172.2 %all-reduce.5.cloned.1.call-start = ((), (), s32[]{:S(2)}) async-start(), calls=%async_computation.1 | async-start | bytes 4194304 | tf_op jit(solution)/shard_map/psum | solution.py:527
  83.1 2.2 copy-start.1
  150.8 1.3 copy-start.2
  254.0 1.3 copy-start.3
  257.1 75.4 %copy-start.4 = (f32[2048,256]{1,0:T(8,128)S(1)}, f32[2048,256]{1,0:T(8,128)}, u32[]{:S(2)}) copy-start(f32[2048,256]{1,0:T(8,128)} %copy-done.3) | copy-start | bytes 6291460
Sparse Core Ops, SparseCore 0:
  83.2 67.9 all-reduce.2
  157.0 84.0 all-reduce.4

commit v3 on v2

--- a/solution.py
+++ b/solution.py
@@ -10,7 +10,7 @@
 GROUPS = 2
 CHUNKS = 32
 SKEW = 3
-BLOCKS = 4
+BLOCKS = 8
 EACH = CHUNKS // BLOCKS
 VMEM_LIMIT = 40 * 1024 * 1024
 
@@ -65,8 +65,6 @@
     def _():
         signal(barrier, up)
 
-    pl.semaphore_wait(barrier, 1 + has_down.astype(jnp.int32) + has_up.astype(jnp.int32))
-
     block = EACH * chunk
 
     def block_rows(q):
@@ -80,6 +78,8 @@
     load(0).start()
     load(1).start()
     g_ref[...] = jnp.zeros_like(g_ref)
+
+    pl.semaphore_wait(barrier, 1 + has_down.astype(jnp.int32) + has_up.astype(jnp.int32))
 
     def accumulate(q):
         load(q).wait()
@@ -90,9 +90,13 @@
         def _():
             load(q + 2).start()
 
-    swap = remote(x_ref.at[pl.ds(other, half)], ex, ex_send, ex_recv, sibling)
-    swap.start()
-    swap.wait()
+    def swap(b):
+        rows = pl.ds(pl.multiple_of(b * block, block), block)
+        source = pl.ds(pl.multiple_of(other + b * block, block), block)
+        return remote(x_ref.at[source], ex.at[rows], ex_send.at[b], ex_recv.at[b], sibling)
+
+    for b in range(BLOCKS):
+        swap(b).start()
 
     def rows_of(i):
         return pl.ds(pl.multiple_of(i * chunk, chunk), chunk)
@@ -129,6 +133,10 @@
     last = jnp.maximum(z, line - 1 - z)
 
     def step(t, carry):
+        @pl.when((t % EACH == 0) & (t < CHUNKS))
+        def _():
+            swap(t // EACH).wait_recv()
+
         i = t - SKEW * z
 
         @pl.when((i >= 0) & (i < CHUNKS))
@@ -183,6 +191,8 @@
     lax.fori_loop(0, CHUNKS + SKEW * (line - 1), step, 0)
 
     accumulate_side(BLOCKS - 1)
+    for b in range(BLOCKS):
+        swap(b).wait_send()
 
     def finish(i, carry):
         @pl.when(has_up)
@@ -216,7 +226,7 @@
             pltpu.SemaphoreType.DMA((2,)),
         ]
         + [buffer] * 3
-        + [pltpu.SemaphoreType.DMA] * 2
+        + [pltpu.SemaphoreType.DMA((BLOCKS,))] * 2
         + [pltpu.SemaphoreType.DMA((CHUNKS,))] * 6,
         compiler_params=pltpu.CompilerParams(
             collective_id=1, has_side_effects=True, vmem_limit_bytes=VMEM_LIMIT
@@ -273,11 +283,6 @@
         def _():
             signal(barrier, {"row": z})
 
-    if square:
-        pl.semaphore_wait(barrier, jnp.where(is_far, 2, 3))
-    else:
-        pl.semaphore_wait(barrier, jnp.where(is_root, line, 2))
-
     block = EACH * chunk
 
     def load(q):
@@ -307,6 +312,12 @@
     load(1).start()
     g_high[...], g_low[...] = parts_of(g_ref[...])
     multiply(0, p_other)
+
+    if square:
+        pl.semaphore_wait(barrier, jnp.where(is_far, 2, 3))
+    else:
+        pl.semaphore_wait(barrier, jnp.where(is_root, line, 2))
+
     swap(0).start()
     multiply(1, p_own)
 

time: 345 us -> 325 us (0.942)
  Pallas kernels: 305 us -> 280 us
  waiting for transfers between devices: 0.04 us -> 3.92 us
    pallas_call x2, Pallas kernels: 172 us -> 157 us  [collect(): pl.pallas_call(functools.partial(collect_kernel, line, chunk), out_shape=...]
    pallas_call x2, Pallas kernels: 133 us -> 123 us  [spread(): pl.pallas_call(functools.partial(spread_kernel, line, chunk), out_shape=j...]
    psum x2, waiting for transfers between devices: 0.01 us -> 3.89 us  [per_device(): lax.psum(partials[g], 'row').T / order]
  transfers between devices with their start and end apart: 2 -> 2, of which waited for: 0 -> 1; matrix products, arithmetic and copies ran while one was open for 0% -> 0% of each run, Pallas kernels for 47% -> 47%
where the time goes in v3:
time: 325 us; the launch traced here: 324 us
  Pallas kernels  280 us (86%)
  between operations  15 us (5%)
  other arithmetic  9.6 us (3%)
  local copies, waits for them, and re-layouts  9.56 us (3%)
  matrix products  5.66 us (2%)
  waiting for transfers between devices  3.92 us (1%)
    pallas_call x2, Pallas kernels, collect(): pl.pallas_call(functools.partial(collect_kernel, line, chunk), out_shape=...  157 us
    pallas_call x2, Pallas kernels, spread(): pl.pallas_call(functools.partial(spread_kernel, line, chunk), out_shape=j...  123 us
  transfers between devices with their start and end apart: 2, of which 1 were waited for; matrix products, arithmetic and copies ran while one was open for 0% of the time, Pallas kernels for 47%

profile of v3, /device:TPU:6, one launch (start us, length us, event | category | flops | bytes accessed | tf_op | source)
XLA Modules:
  0.0 323.9 jit_solution(15884322301669781168)
XLA Ops:
  6.5 0.0 copy-start
  6.5 0.0 all-reduce.3.cloned.1.call-start
  7.3 6.0 %dynamic-slice_select_fusion = (f32[4096,256]{1,0:T(8,128)S(1)}, f32[4096,256]{1,0:T(8,128)}) fusion(f32[4096,2048]{1,0:T(8,128)} %a_ref.7, s32[]{:T(128)S(6)} %select_n.31, pred[]{:T(512)S(6)} %eq.52, s32[]{:T(128)S(6)} %select_n.29), kind=kLoop, calls=%fused_computation.5 | loop fusion | flops 2097152 | bytes 16777224 | tf_op jit(solution)/shard_map/jit(_where)/select_n | solution.py:530
  13.4 62.0 %spread_panel.2 = f32[256,2048]{1,0:T(8,128)S(1)} custom-call(f32[4096,256]{1,0:T(8,128)S(1)} %get-tuple-element.13.x_ref, f32[4096,2048]{1,0:T(8,128)} %a_ref.7), custom_call_target="tpu_custom_call" | custom-call | flops 12884901888 | bytes 220000000 | tf_op jit(solution)/shard_map/spread_panel/pallas_call | solution.py:218
  75.4 1.8 copy.5
  77.2 0.0 all-reduce.3.cloned.1.call-update
  77.3 0.0 all-reduce.5.cloned.1.call-start
  77.3 0.0 copy-start.1
  77.3 2.2 copy-done.1
  79.5 60.8 %spread_panel.3 = f32[256,2048]{1,0:T(8,128)S(1)} custom-call(f32[4096,256]{1,0:T(8,128)S(1)} %copy-done.1, f32[4096,2048]{1,0:T(8,128)} %a_ref.7), custom_call_target="tpu_custom_call" | custom-call | flops 12884901888 | bytes 220000000 | tf_op jit(solution)/shard_map/spread_panel/pallas_call | solution.py:218
  140.3 0.0 copy-start.2
  140.3 1.3 copy-done.2
  141.7 3.9 %all-reduce.3.cloned.1.call-done = f32[256,2048]{0,1:T(8,128)} async-done(((f32[256,2048]{0,1:T(8,128)}), f32[256,2048]{0,1:T(8,128)}) %all-reduce.3.cloned.1.call-update) | async-done | bytes 2097168 | tf_op jit(solution)/shard_map/psum | solution.py:538
  145.5 1.8 bitcast_add_fusion.1.g_ref
  147.3 2.9 copy.6
  150.2 0.0 all-reduce.5.cloned.1.call-update
  150.9 89.9 %collect_product.2 = f32[2048,256]{1,0:T(8,128)S(1)} custom-call(f32[2048,256]{1,0:T(8,128)S(1)} %bitcast_add_fusion.1.g_ref, f32[4096,2048]{1,0:T(8,128)} %a_ref.7), custom_call_target="tpu_custom_call" | custom-call | flops 12884901888 | bytes 220000000 | tf_op jit(solution)/shard_map/collect_product/pallas_call | solution.py:478
  240.8 0.0 copy-start.3
  240.9 1.3 copy-done.3
  242.2 0.0 all-reduce.5.cloned.1.call-done
  242.2 1.8 bitcast_add_fusion.g_ref
  243.9 0.0 copy-start.4
  243.9 67.4 %collect_product.3 = f32[2048,256]{1,0:T(8,128)S(1)} custom-call(f32[2048,256]{1,0:T(8,128)S(1)} %bitcast_add_fusion.g_ref, f32[4096,2048]{1,0:T(8,128)} %a_ref.7), custom_call_target="tpu_custom_call" | custom-call | flops 12884901888 | bytes 220000000 | tf_op jit(solution)/shard_map/collect_product/pallas_call | solution.py:478
  311.4 0.0 copy-done
  311.4 0.0 copy-done.4
  311.4 5.7 %multiply_select_fusion = f32[2048,512]{1,0:T(8,128)} fusion(f32[512,512]{1,0:T(8,128)S(1)} %copy-done, f32[2048,256]{1,0:T(8,128)S(1)} %collect_product.3, f32[2048,256]{1,0:T(8,128)S(1)} %copy-done.4, s32[512]{0:T(512)S(1)} %iota_add_fusion.1, s32[2048]{0:T(1024)S(1)} %iota_add_fusion, pred[2048]{0:T(1024)(128)(4,1)S(1)} %compare_compare_fusion), kind=kOutput, calls=%fused_computation.4 | convolution fusion | flops 3227516928 | bytes 9449472 | tf_op jit(solution)/shard_map/dot_general | solution.py:502
  (5 shorter events, 0.0 us)
Async XLA Ops:
  6.5 304.8 %copy-start = (f32[512,512]{1,0:T(8,128)S(1)}, f32[512,512]{1,0:T(8,128)}, u32[]{:S(2)}) copy-start(f32[512,512]{1,0:T(8,128)} %param.5) | copy-start | bytes 3145732
  6.5 139.0 %all-reduce.3.cloned.1.call-start = ((), (), s32[]{:S(2)}) async-start(), calls=%async_computation | async-start | bytes 4194304 | tf_op jit(solution)/shard_map/psum | solution.py:538
  77.3 164.9 %all-reduce.5.cloned.1.call-start = ((), (), s32[]{:S(2)}) async-start(), calls=%async_computation.1 | async-start | bytes 4194304 | tf_op jit(solution)/shard_map/psum | solution.py:538
  77.3 2.2 copy-start.1
  140.3 1.3 copy-start.2
  240.8 1.3 copy-start.3
  243.9 67.4 %copy-start.4 = (f32[2048,256]{1,0:T(8,128)S(1)}, f32[2048,256]{1,0:T(8,128)}, u32[]{:S(2)}) copy-start(f32[2048,256]{1,0:T(8,128)} %copy-done.3) | copy-start | bytes 6291460
Sparse Core Ops, SparseCore 0:
  77.4 68.1 all-reduce.2
  150.4 89.1 all-reduce.4

commit v4 on v3

--- a/solution.py
+++ b/solution.py
@@ -9,7 +9,7 @@
 
 GROUPS = 2
 CHUNKS = 32
-SKEW = 3
+SKEW = 2
 BLOCKS = 8
 EACH = CHUNKS // BLOCKS
 VMEM_LIMIT = 40 * 1024 * 1024

time: 325 us -> 351 us (1.080)
  Pallas kernels: 280 us -> 310 us
  waiting for transfers between devices: 3.92 us -> 0.04 us
    pallas_call x2, Pallas kernels: 123 us -> 141 us  [spread(): pl.pallas_call(functools.partial(spread_kernel, line, chunk), out_shape=j...]
    pallas_call x2, Pallas kernels: 157 us -> 169 us  [collect(): pl.pallas_call(functools.partial(collect_kernel, line, chunk), out_shape=...]
    psum x2, waiting for transfers between devices: 3.89 us -> 0.01 us  [per_device(): lax.psum(partials[g], 'row').T / order]
  transfers between devices with their start and end apart: 2 -> 2, of which waited for: 1 -> 0; matrix products, arithmetic and copies ran while one was open for 0% -> 0% of each run, Pallas kernels for 47% -> 47%
where the time goes in v4:
time: 351 us; the launch traced here: 350 us
  Pallas kernels  310 us (88%)
  between operations  15 us (4%)
  other arithmetic  9.6 us (3%)
  local copies, waits for them, and re-layouts  9.56 us (3%)
  matrix products  5.67 us (2%)
    pallas_call x2, Pallas kernels, collect(): pl.pallas_call(functools.partial(collect_kernel, line, chunk), out_shape=...  169 us
    pallas_call x2, Pallas kernels, spread(): pl.pallas_call(functools.partial(spread_kernel, line, chunk), out_shape=j...  141 us
  transfers between devices with their start and end apart: 2, of which 0 were waited for; matrix products, arithmetic and copies ran while one was open for 0% of the time, Pallas kernels for 47%

profile of v4, /device:TPU:6, one launch (start us, length us, event | category | flops | bytes accessed | tf_op | source)
XLA Modules:
  0.0 350.1 jit_solution(11266218721600348353)
XLA Ops:
  6.5 0.0 copy-start
  6.5 0.0 all-reduce.3.cloned.1.call-start
  7.3 6.0 %dynamic-slice_select_fusion = (f32[4096,256]{1,0:T(8,128)S(1)}, f32[4096,256]{1,0:T(8,128)}) fusion(f32[4096,2048]{1,0:T(8,128)} %a_ref.7, s32[]{:T(128)S(6)} %select_n.31, pred[]{:T(512)S(6)} %eq.52, s32[]{:T(128)S(6)} %select_n.29), kind=kLoop, calls=%fused_computation.5 | loop fusion | flops 2097152 | bytes 16777224 | tf_op jit(solution)/shard_map/jit(_where)/select_n | solution.py:530
  13.4 71.0 %spread_panel.2 = f32[256,2048]{1,0:T(8,128)S(1)} custom-call(f32[4096,256]{1,0:T(8,128)S(1)} %get-tuple-element.13.x_ref, f32[4096,2048]{1,0:T(8,128)} %a_ref.7), custom_call_target="tpu_custom_call" | custom-call | flops 12884901888 | bytes 220000000 | tf_op jit(solution)/shard_map/spread_panel/pallas_call | solution.py:218
  84.3 1.8 copy.5
  86.2 0.0 all-reduce.3.cloned.1.call-update
  86.2 0.0 all-reduce.5.cloned.1.call-start
  86.3 0.0 copy-start.1
  86.3 2.2 copy-done.1
  88.5 70.2 %spread_panel.3 = f32[256,2048]{1,0:T(8,128)S(1)} custom-call(f32[4096,256]{1,0:T(8,128)S(1)} %copy-done.1, f32[4096,2048]{1,0:T(8,128)} %a_ref.7), custom_call_target="tpu_custom_call" | custom-call | flops 12884901888 | bytes 220000000 | tf_op jit(solution)/shard_map/spread_panel/pallas_call | solution.py:218
  158.7 0.0 copy-start.2
  158.7 1.3 copy-done.2
  160.0 0.0 all-reduce.3.cloned.1.call-done
  160.0 1.8 bitcast_add_fusion.1.g_ref
  161.8 2.9 copy.6
  164.7 0.0 all-reduce.5.cloned.1.call-update
  165.4 93.7 %collect_product.2 = f32[2048,256]{1,0:T(8,128)S(1)} custom-call(f32[2048,256]{1,0:T(8,128)S(1)} %bitcast_add_fusion.1.g_ref, f32[4096,2048]{1,0:T(8,128)} %a_ref.7), custom_call_target="tpu_custom_call" | custom-call | flops 12884901888 | bytes 220000000 | tf_op jit(solution)/shard_map/collect_product/pallas_call | solution.py:478
  259.2 0.0 copy-start.3
  259.2 1.3 copy-done.3
  260.5 0.0 all-reduce.5.cloned.1.call-done
  260.5 1.8 bitcast_add_fusion.g_ref
  262.3 0.0 copy-start.4
  262.3 75.3 %collect_product.3 = f32[2048,256]{1,0:T(8,128)S(1)} custom-call(f32[2048,256]{1,0:T(8,128)S(1)} %bitcast_add_fusion.g_ref, f32[4096,2048]{1,0:T(8,128)} %a_ref.7), custom_call_target="tpu_custom_call" | custom-call | flops 12884901888 | bytes 220000000 | tf_op jit(solution)/shard_map/collect_product/pallas_call | solution.py:478
  337.6 0.0 copy-done
  337.6 0.0 copy-done.4
  337.6 5.7 %multiply_select_fusion = f32[2048,512]{1,0:T(8,128)} fusion(f32[512,512]{1,0:T(8,128)S(1)} %copy-done, f32[2048,256]{1,0:T(8,128)S(1)} %collect_product.3, f32[2048,256]{1,0:T(8,128)S(1)} %copy-done.4, s32[512]{0:T(512)S(1)} %iota_add_fusion.1, s32[2048]{0:T(1024)S(1)} %iota_add_fusion, pred[2048]{0:T(1024)(128)(4,1)S(1)} %compare_compare_fusion), kind=kOutput, calls=%fused_computation.4 | convolution fusion | flops 3227516928 | bytes 9449472 | tf_op jit(solution)/shard_map/dot_general | solution.py:502
  (5 shorter events, 0.0 us)
Async XLA Ops:
  6.5 331.0 %copy-start = (f32[512,512]{1,0:T(8,128)S(1)}, f32[512,512]{1,0:T(8,128)}, u32[]{:S(2)}) copy-start(f32[512,512]{1,0:T(8,128)} %param.5) | copy-start | bytes 3145732
  6.5 153.5 %all-reduce.3.cloned.1.call-start = ((), (), s32[]{:S(2)}) async-start(), calls=%async_computation | async-start | bytes 4194304 | tf_op jit(solution)/shard_map/psum | solution.py:538
  86.2 174.3 %all-reduce.5.cloned.1.call-start = ((), (), s32[]{:S(2)}) async-start(), calls=%async_computation.1 | async-start | bytes 4194304 | tf_op jit(solution)/shard_map/psum | solution.py:538
  86.3 2.2 copy-start.1
  158.7 1.3 copy-start.2
  259.2 1.3 copy-start.3
  262.3 75.3 %copy-start.4 = (f32[2048,256]{1,0:T(8,128)S(1)}, f32[2048,256]{1,0:T(8,128)}, u32[]{:S(2)}) copy-start(f32[2048,256]{1,0:T(8,128)} %copy-done.3) | copy-start | bytes 6291460
Sparse Core Ops, SparseCore 0:
  86.3 67.3 all-reduce.2
  164.9 85.4 all-reduce.4
